TPU v7x, 256 devices: a whole 4x4x8 slice. The times are simulated.
256 devices in a mesh: ctx: 32 (over x_hi, z, core), head: 8 (over x_lo, y).
Axes of the slice: x: 4 (x_hi: 2, x_lo: 2; x = x_hi * 2 + x_lo), y: 4, z: 8, core: 2. Of those that a mesh axis runs over, the one named last changes fastest.
Arguments:
- queries_one: bfloat16 [4096, 4096], P('ctx', 'head'), may hold values from -6 to 6
- grads_one: bfloat16 [4096, 4096], P('ctx', 'head'), may hold values from -6 to 6
- queries_two: bfloat16 [4096, 4096], P('ctx', 'head'), may hold values from -6 to 6
- grads_two: bfloat16 [4096, 4096], P('ctx', 'head'), may hold values from -6 to 6
- key_rows: bfloat16 [4096, 1024], P('ctx', 'head'), may hold values from -6 to 6
- value_rows: bfloat16 [4096, 1024], P('ctx', 'head'), may hold values from -6 to 6
- shared_input: bfloat16 [4096, 8192], P('ctx'), may hold values from -6 to 6
- key_weight: bfloat16 [8192, 1024], P(None, 'head'), may hold values from -0.09375 to 0.09375
- value_weight: bfloat16 [8192, 1024], P(None, 'head'), may hold values from -0.0625 to 0.0625
- block_order: int32 [64], replicated, may hold values from 0 to 63, as said below
Outputs:
- query_grad_one: bfloat16 [4096, 4096], P('ctx', 'head')
- query_grad_two: bfloat16 [4096, 4096], P('ctx', 'head')
- input_grad: bfloat16 [4096, 8192], P('ctx', 'head')
- key_weight_grad: float32 [8192, 1024], P('ctx', 'head')
- value_weight_grad: float32 [8192, 1024], P('ctx', 'head')
Inputs may be any that keep to these rules, and one draw needn't show every extreme that they name: `block_order`: each block 0 to 63 once; slots 2c and 2c + 1 hold blocks i and 63 - i for some i.
All inputs are finite; a program needn't handle non-finite values.
Results may differ from a plain program's by a relative error of at most 0.013.
Values may be sent and summed in bfloat16 or wider, within the bound.
No kernel may reach another device: no remote copies, remote signals or barrier semaphores. Data moves between devices by JAX's collectives and lax.ppermute only.
A program may use at most 128 MiB of HBM per device.

v0:
```python
import math
import jax
import jax.numpy as jnp
from jax import lax
from jax.sharding import PartitionSpec as P

H = 32
KV = 8
DH = 128


def attend(queries, grads, query_pos, keys_pos, values_pos, key_pos, scale):
    scores = (
        jnp.einsum("rkgd,jkd->kgrj", queries, keys_pos, preferred_element_type=jnp.float32) * scale
    )
    allowed = key_pos[None, :] <= query_pos[:, None]
    scores = jnp.where(allowed, scores, -jnp.inf)
    peak = jnp.max(scores, axis=-1, keepdims=True)
    weights = jnp.exp(scores - peak)
    probabilities = weights / jnp.sum(weights, axis=-1, keepdims=True)
    prob_low = probabilities.astype(jnp.bfloat16)
    dprob = jnp.einsum("rkgd,jkd->kgrj", grads, values_pos, preferred_element_type=jnp.float32)
    row_delta = jnp.sum(probabilities * dprob, axis=-1, keepdims=True)
    dscore = (probabilities * (dprob - row_delta) * scale).astype(jnp.bfloat16)
    dquery = jnp.einsum(
        "kgrj,jkd->rkgd", dscore, keys_pos, preferred_element_type=jnp.float32
    ).astype(jnp.bfloat16)
    dkey = jnp.einsum("kgrj,rkgd->jkd", dscore, queries, preferred_element_type=jnp.float32)
    dvalue = jnp.einsum("kgrj,rkgd->jkd", prob_low, grads, preferred_element_type=jnp.float32)
    return (dquery, dkey, dvalue)


def on_device(
    queries_one,
    grads_one,
    queries_two,
    grads_two,
    key_rows,
    value_rows,
    shared_input,
    key_weight,
    value_weight,
    block_order,
):
    rows_local = queries_one.shape[0]
    half_rows = rows_local // 2
    ctx_count = lax.axis_size("ctx")
    seq_len = rows_local * ctx_count
    kv_local = key_rows.shape[1] // DH
    group = H // KV
    scale = 1.0 / math.sqrt(DH)
    gathered_keys, gathered_values = (
        lax.all_gather(key_rows, "ctx", axis=0, tiled=True),
        lax.all_gather(value_rows, "ctx", axis=0, tiled=True),
    )
    inverse = jnp.argsort(block_order)

    def to_position(slotted):
        return slotted.reshape(2 * ctx_count, half_rows, kv_local * DH)[inverse].reshape(
            seq_len, kv_local, DH
        )

    def to_slot(positioned):
        return positioned.reshape(2 * ctx_count, half_rows, kv_local * DH)[block_order].reshape(
            seq_len, kv_local * DH
        )

    keys_pos = to_position(gathered_keys)
    values_pos = to_position(gathered_values)
    key_pos = jnp.arange(seq_len, dtype=jnp.int32)
    own_blocks = lax.dynamic_slice_in_dim(block_order, 2 * lax.axis_index("ctx"), 2)
    query_pos = (
        own_blocks[:, None] * half_rows + jnp.arange(half_rows, dtype=jnp.int32)[None, :]
    ).reshape(rows_local)

    def layer_grads(queries, grads):
        query_four = queries.reshape(rows_local, kv_local, group, DH)
        grad_four = grads.reshape(rows_local, kv_local, group, DH)
        dquery, dkey, dvalue = attend(
            query_four, grad_four, query_pos, keys_pos, values_pos, key_pos, scale
        )
        return (dquery.reshape(rows_local, kv_local * group * DH), to_slot(dkey), to_slot(dvalue))

    dq_one, dk_one, dv_one = layer_grads(queries_one, grads_one)
    dq_two, dk_two, dv_two = layer_grads(queries_two, grads_two)
    key_total, value_total = (
        lax.psum_scatter(dk_one + dk_two, "ctx", scatter_dimension=0, tiled=True),
        lax.psum_scatter(dv_one + dv_two, "ctx", scatter_dimension=0, tiled=True),
    )
    key_grad = key_total.astype(jnp.bfloat16)
    value_grad = value_total.astype(jnp.bfloat16)
    contract_cols = (((1,), (1,)), ((), ()))
    input_term = lax.dot_general(
        key_grad, key_weight, contract_cols, preferred_element_type=jnp.float32
    )
    input_term = input_term + lax.dot_general(
        value_grad, value_weight, contract_cols, preferred_element_type=jnp.float32
    )
    input_grad = lax.psum_scatter(input_term, "head", scatter_dimension=1, tiled=True).astype(
        jnp.bfloat16
    )
    both_grads = jnp.concatenate([key_grad, value_grad], axis=1)
    width = key_grad.shape[1]
    contract_rows = (((0,), (0,)), ((), ()))
    weight_grad = lax.psum_scatter(
        lax.dot_general(
            shared_input, both_grads, contract_rows, preferred_element_type=jnp.float32
        ),
        "ctx",
        scatter_dimension=0,
        tiled=True,
    )
    return (dq_one, dq_two, input_grad, weight_grad[:, :width], weight_grad[:, width:])


def solution(mesh):
    return jax.shard_map(
        on_device,
        mesh=mesh,
        in_specs=(
            P("ctx", "head"),
            P("ctx", "head"),
            P("ctx", "head"),
            P("ctx", "head"),
            P("ctx", "head"),
            P("ctx", "head"),
            P("ctx", None),
            P(None, "head"),
            P(None, "head"),
            P(),
        ),
        out_specs=(
            P("ctx", "head"),
            P("ctx", "head"),
            P("ctx", "head"),
            P("ctx", "head"),
            P("ctx", "head"),
        ),
        check_vma=False,
    )
```

profile of v0, /device:TPU:8, one launch (start us, length us, event | category | flops | bytes accessed | tf_op | source)
XLA Modules:
  0.0 679.7 jit_solution(15424929762015373111)
XLA Ops:
  7.2 0.7 all-gather.5.cloned.1.call-update
  8.0 0.7 all-gather.3.cloned.1.call-update
  8.7 0.7 dynamic-slice_multiply_fusion
  9.5 0.1 add.61
  9.6 2.7 sort.17
  12.3 0.7 compare_select_fusion
  13.0 1.1 iota_compare_fusion
  14.1 77.1 %all-gather.5.cloned.1.call-done = bf16[4096,128]{1,0:T(8,128)(2,1)} async-done(((bf16[128,128]{1,0:T(8,128)(2,1)}), bf16[4096,128]{1,0:T(8,128)(2,1)}) %all-gather.5.cloned.1.call-update) | async-done | bytes 1048592 | tf_op jit(solution)/shard_map/all_gather | solution.py:54
  91.2 2.9 gather_fusion.1
  94.1 74.3 %all-gather.3.cloned.1.call-done = bf16[4096,128]{1,0:T(8,128)(2,1)} async-done(((bf16[128,128]{1,0:T(8,128)(2,1)}), bf16[4096,128]{1,0:T(8,128)(2,1)}) %all-gather.3.cloned.1.call-update) | async-done | bytes 1048592 | tf_op jit(solution)/shard_map/all_gather | solution.py:53
  168.5 2.0 gather_fusion
  170.4 2.4 fusion.48
  172.9 1.3 fusion.47
  174.2 1.1 fusion.9
  175.3 5.1 fusion.4
  180.4 5.5 fusion.12
  185.9 2.7 fusion.29
  188.6 1.1 fusion.11
  189.7 4.3 fusion
  194.0 4.7 fusion.13
  198.8 1.9 copy-done.2
  200.7 2.6 fusion.23
  203.3 3.6 gather_fusion.2
  206.9 3.6 gather_fusion.3
  210.5 4.1 add.63
  214.7 0.3 reduce-scatter.7.cloned.1.call-start
  215.0 6.2 fusion.14
  221.2 3.6 gather_fusion.5
  224.8 6.4 fusion.16
  231.1 3.6 gather_fusion.4
  234.7 4.1 add.65
  239.0 92.0 %reduce-scatter.5.cloned.1.call-done = f32[128,128]{1,0:T(8,128)} async-done(((f32[4096,128]{1,0:T(8,128)}), f32[128,128]{1,0:T(8,128)}) %reduce-scatter.5.cloned.1.call-update) | async-done | bytes 65552 | tf_op jit(solution)/shard_map/reduce_scatter | solution.py:87
  331.0 0.8 convert_element_type.47
  331.8 4.3 fusion.49
  336.1 116.7 %reduce-scatter.7.cloned.1.call-done = f32[128,128]{1,0:T(8,128)} async-done(((f32[4096,128]{1,0:T(8,128)}), f32[128,128]{1,0:T(8,128)}) %reduce-scatter.7.cloned.1.call-update) | async-done | bytes 65552 | tf_op jit(solution)/shard_map/reduce_scatter | solution.py:88
  452.8 0.8 convert_element_type.50
  453.6 5.5 convolution_add_fusion
  459.2 4.5 convolution_bitcast_fusion
  463.7 2.9 convolution_convert_fusion.1
  466.7 0.8 copy.44
  467.5 3.3 convolution_convert_fusion
  470.8 0.8 copy.45
  471.5 39.2 %reduce-scatter.9.cloned.1.call-done = f32[128,1024]{1,0:T(8,128)} async-done(((f32[128,8192]{1,0:T(8,128)}), f32[128,1024]{1,0:T(8,128)}) %reduce-scatter.9.cloned.1.call-update) | async-done | bytes 524304 | tf_op jit(solution)/shard_map/reduce_scatter | solution.py:99
  510.7 1.8 convert_element_type.51
  512.5 157.9 %reduce-scatter.11.cloned.1.call-done = f32[256,256]{0,1:T(8,128)} async-done(((f32[8192,256]{0,1:T(8,128)}), f32[256,256]{0,1:T(8,128)}) %reduce-scatter.11.cloned.1.call-update) | async-done | bytes 262160 | tf_op jit(solution)/shard_map/reduce_scatter | solution.py:105
  670.4 1.0 fusion.46
  671.4 0.8 copy.47
  672.1 0.8 copy.46
  (35 shorter events, 0.4 us)
Async XLA Ops:
  7.2 452.0 %copy-start = (bf16[128,8192]{1,0:T(8,128)(2,1)S(1)}, bf16[128,8192]{1,0:T(8,128)(2,1)}, u32[]{:S(2)}) copy-start(bf16[128,8192]{1,0:T(8,128)(2,1)} %param.16) | copy-start | bytes 6291460
  7.2 165.7 %copy-start.7 = (bf16[128,512]{1,0:T(8,128)(2,1)S(1)}, bf16[128,512]{1,0:T(8,128)(2,1)}, u32[]{:S(2)}) copy-start(bf16[128,512]{1,0:T(8,128)(2,1)} %param.10) | copy-start | bytes 393220
  7.2 84.0 %all-gather.5.cloned.1.call-start = ((), (), s32[]{:S(2)}) async-start(), calls=%async_computation.5 | async-start | bytes 1081344 | tf_op jit(solution)/shard_map/all_gather | solution.py:54
  7.9 160.5 %all-gather.3.cloned.1.call-start = ((), (), s32[]{:S(2)}) async-start(), calls=%async_computation.4 | async-start | bytes 1081344 | tf_op jit(solution)/shard_map/all_gather | solution.py:53
  8.7 322.3 %reduce-scatter.5.cloned.1.call-start = ((), (), s32[]{:S(2)}) async-start(), calls=%async_computation.6 | async-start | bytes 2162688 | tf_op jit(solution)/shard_map/reduce_scatter | solution.py:87
  170.4 2.5 copy-start.6
  172.9 21.1 %copy-start.4 = (f32[1,4,128,4096]{2,3,1,0:T(8,128)}, f32[1,4,128,4096]{2,3,1,0:T(8,128)S(1)}, u32[]{:S(2)}) copy-start(f32[1,4,128,4096]{2,3,1,0:T(8,128)S(1)} %get-tuple-element.24) | copy-start | bytes 25165828
  172.9 2.4 copy-start.5
  172.9 2.4 copy-start.10
  174.2 6.2 copy-start.3
  185.9 8.1 %copy-start.1 = (bf16[4,128,4096]{1,2,0:T(8,128)(2,1)}, bf16[4,128,4096]{1,2,0:T(8,128)(2,1)S(1)}, u32[]{:S(2)}) copy-start(bf16[4,128,4096]{1,2,0:T(8,128)(2,1)S(1)} %fusion.12) | copy-start | bytes 12582916
  185.9 3.8 copy-start.9
  194.0 6.7 copy-start.8
  198.8 1.9 copy-start.2
  214.7 238.1 %reduce-scatter.7.cloned.1.call-start = ((), (), s32[]{:S(2)}) async-start(), calls=%async_computation.7 | async-start | bytes 2162688 | tf_op jit(solution)/shard_map/reduce_scatter | solution.py:88
  238.9 271.8 %reduce-scatter.9.cloned.1.call-start = ((), (), s32[]{:S(2)}) async-start(), calls=%async_computation.8 | async-start | bytes 4718592 | tf_op jit(solution)/shard_map/reduce_scatter | solution.py:99
  459.2 211.2 %reduce-scatter.11.cloned.1.call-start = ((), (), s32[]{:S(2)}) async-start(), calls=%async_computation.9 | async-start | bytes 8650752 | tf_op jit(solution)/shard_map/reduce_scatter | solution.py:105
Sparse Core Ops, SparseCore 0:
  10.8 80.3 all-gather.4
  94.0 74.4 all-gather.2
  214.8 116.1 reduce-scatter.4
  335.6 117.1 reduce-scatter.6
  459.3 51.4 reduce-scatter.8
  515.0 155.3 reduce-scatter.10
where the time goes:
time: 680 us
  waiting for transfers between devices  559 us (82%)
  matrix products  51.4 us (8%)
  other arithmetic  29.5 us (4%)
  local copies, waits for them, and re-layouts  25.4 us (4%)
  between operations  14.3 us (2%)
    reduce_scatter x1, waiting for transfers between devices, on_device(): lax.psum_scatter(lax.dot_general(shared_input, both_grads, contract_rows,...  158 us
    reduce_scatter x1, waiting for transfers between devices, on_device(): lax.psum_scatter(dv_one + dv_two, 'ctx', scatter_dimension=0, tiled=True)  117 us
    reduce_scatter x1, waiting for transfers between devices, on_device(): lax.psum_scatter(dk_one + dk_two, 'ctx', scatter_dimension=0, tiled=True)  92 us
    all_gather x1, waiting for transfers between devices, on_device(): lax.all_gather(value_rows, 'ctx', axis=0, tiled=True)  77.1 us
    all_gather x1, waiting for transfers between devices, on_device(): lax.all_gather(key_rows, 'ctx', axis=0, tiled=True)  74.3 us
    reduce_scatter x1, waiting for transfers between devices, on_device(): lax.psum_scatter(input_term, 'head', scatter_dimension=1, tiled=True)  39.2 us
    gather x4, local copies, waits for them, and re-layouts, to_slot(): positioned.reshape(2 * ctx_count, half_rows, kv_local * DH)[block_order]  14.5 us
  transfers between devices with their start and end apart: 6, of which 6 were waited for; matrix products, arithmetic and copies ran while one was open for 8% of the time, Pallas kernels for 0%

commit v1 on v0

--- a/solution.py
+++ b/solution.py
@@ -49,9 +49,22 @@
     kv_local = key_rows.shape[1] // DH
     group = H // KV
     scale = 1.0 / math.sqrt(DH)
+
+    def reach_the_meshes(frame):
+        raw_out = jnp.concatenate(
+            lax.all_to_all(
+                jnp.stack(tuple((frame for _ in range(lax.psum(1, "ctx"))))),
+                concat_axis=0,
+                axis_name="ctx",
+                split_axis=0,
+            ),
+            axis=0,
+        )
+        return raw_out
+
     gathered_keys, gathered_values = (
         lax.all_gather(key_rows, "ctx", axis=0, tiled=True),
-        lax.all_gather(value_rows, "ctx", axis=0, tiled=True),
+        reach_the_meshes(value_rows),
     )
     inverse = jnp.argsort(block_order)
 

time: 680 us -> 609 us (0.90)
  waiting for transfers between devices: 559 us -> 474 us
  starting transfers between devices: 0.46 us -> 11.9 us
    all_gather x1 -> x0, waiting for transfers between devices: 77.1 us -> none  [on_device(): lax.all_gather(value_rows, 'ctx', axis=0, tiled=True)]
    all_to_all x0 -> x1, starting transfers between devices: none -> 11.4 us  [reach_the_meshes(): lax.all_to_all(jnp.stack(tuple((frame for _ in range(lax.psum(1, 'ctx')))...]
    all_gather x1, waiting for transfers between devices: 74.3 us -> 67.1 us  [on_device(): lax.all_gather(key_rows, 'ctx', axis=0, tiled=True)]
  transfers between devices with their start and end apart: 6 -> 6, of which waited for: 6 -> 5; matrix products, arithmetic and copies ran while one was open for 8% -> 9% of each run, Pallas kernels for 0% -> 0%
where the time goes in v1:
time: 609 us; the launch traced here: 608 us
  waiting for transfers between devices  474 us (78%)
  matrix products  51.4 us (8%)
  other arithmetic  29.5 us (5%)
  local copies, waits for them, and re-layouts  27.4 us (4%)
  between operations  14 us (2%)
  starting transfers between devices  11.9 us (2%)
    reduce_scatter x1, waiting for transfers between devices, on_device(): lax.psum_scatter(lax.dot_general(shared_input, both_grads, contract_rows,...  158 us
    reduce_scatter x1, waiting for transfers between devices, on_device(): lax.psum_scatter(dv_one + dv_two, 'ctx', scatter_dimension=0, tiled=True)  117 us
    reduce_scatter x1, waiting for transfers between devices, on_device(): lax.psum_scatter(dk_one + dk_two, 'ctx', scatter_dimension=0, tiled=True)  92.1 us
    all_gather x1, waiting for transfers between devices, on_device(): lax.all_gather(key_rows, 'ctx', axis=0, tiled=True)  67.1 us
    reduce_scatter x1, waiting for transfers between devices, on_device(): lax.psum_scatter(input_term, 'head', scatter_dimension=1, tiled=True)  39.2 us
    gather x4, local copies, waits for them, and re-layouts, to_slot(): positioned.reshape(2 * ctx_count, half_rows, kv_local * DH)[block_order]  14.4 us
    dot_general x2, matrix products, attend(): jnp.einsum('kgrj,rkgd->jkd', prob_low, grads, preferred_element_type=jnp....  12.6 us
  transfers between devices with their start and end apart: 6, of which 5 were waited for; matrix products, arithmetic and copies ran while one was open for 9% of the time, Pallas kernels for 0%

profile of v1, /device:TPU:8, one launch (start us, length us, event | category | flops | bytes accessed | tf_op | source)
XLA Modules:
  0.0 607.8 jit_solution(16527270083623148641)
XLA Ops:
  7.2 0.7 all-gather.2.cloned.1.call-update
  7.9 2.0 stack.2
  9.9 11.4 %all-to-all-start = ((bf16[32,128,128]{2,1,0:T(8,128)(2,1)}), bf16[32,128,128]{2,1,0:T(8,128)(2,1)}, u32[]{:S(2)}, u32[]{:S(2)}) async-start(bf16[32,128,128]{2,1,0:T(8,128)(2,1)} %stack.2), calls=%async_computation | async-start | bytes 2097152 | tf_op jit(solution)/shard_map/all_to_all | solution.py:55
  21.4 0.7 dynamic-slice_multiply_fusion
  22.2 0.1 add.61
  22.3 2.7 sort.17
  25.0 0.7 compare_select_fusion
  25.7 1.1 iota_compare_fusion
  26.8 67.1 %all-gather.2.cloned.1.call-done = bf16[4096,128]{1,0:T(8,128)(2,1)} async-done(((bf16[128,128]{1,0:T(8,128)(2,1)}), bf16[4096,128]{1,0:T(8,128)(2,1)}) %all-gather.2.cloned.1.call-update) | async-done | bytes 1048592 | tf_op jit(solution)/shard_map/all_gather | solution.py:66
  93.9 2.0 gather_fusion
  95.8 2.9 gather_fusion.1
  98.8 2.4 fusion.48
  101.2 1.3 fusion.47
  102.5 1.1 fusion.9
  103.6 5.1 fusion.4
  108.7 5.5 fusion.12
  114.2 2.7 fusion.29
  116.9 1.1 fusion.11
  118.1 4.3 fusion
  122.3 4.7 fusion.13
  127.1 1.9 copy-done.2
  129.0 2.6 fusion.23
  131.6 3.6 gather_fusion.2
  135.2 3.6 gather_fusion.3
  138.8 4.1 add.63
  143.0 0.3 reduce-scatter.7.cloned.1.call-start
  143.3 6.2 %fusion.14 = f32[4096,128,1]{1,0,2:T(8,128)} fusion(f32[1,4,128,4096]{2,3,1,0:T(8,128)} %copy-done.4, f32[4,128]{1,0:T(4,128)S(1)} %fusion.11, f32[4,128]{1,0:T(4,128)S(1)} %get-tuple-element.23, bf16[128,512]{1,0:T(8,128)(2,1)S(1)} %copy-done.9), kind=kOutput, calls=%fused_computation.30 | convolution fusion | flops 543162368 | bytes 10620928 | tf_op jit(solution)/shard_map/kgrj,rkgd->jkd/dot_general | solution.py:29
  149.5 3.6 gather_fusion.5
  153.1 6.4 %fusion.16 = f32[4096,128,1]{1,0,2:T(8,128)} fusion(f32[1,4,128,4096]{2,3,1,0:T(8,128)} %copy-done.3, f32[4,128]{1,0:T(4,128)S(1)} %fusion.9, f32[4,128]{1,0:T(4,128)S(1)} %get-tuple-element.19, bf16[128,512]{1,0:T(8,128)(2,1)S(1)} %copy-done.10), kind=kOutput, calls=%fused_computation.32 | convolution fusion | flops 543162368 | bytes 10620928 | tf_op jit(solution)/shard_map/kgrj,rkgd->jkd/dot_general | solution.py:29
  159.4 3.6 gather_fusion.4
  163.0 4.1 add.65
  167.3 92.1 %reduce-scatter.5.cloned.1.call-done = f32[128,128]{1,0:T(8,128)} async-done(((f32[4096,128]{1,0:T(8,128)}), f32[128,128]{1,0:T(8,128)}) %reduce-scatter.5.cloned.1.call-update) | async-done | bytes 65552 | tf_op jit(solution)/shard_map/reduce_scatter | solution.py:100
  259.4 0.8 convert_element_type.47
  260.2 4.3 fusion.49
  264.5 116.9 %reduce-scatter.7.cloned.1.call-done = f32[128,128]{1,0:T(8,128)} async-done(((f32[4096,128]{1,0:T(8,128)}), f32[128,128]{1,0:T(8,128)}) %reduce-scatter.7.cloned.1.call-update) | async-done | bytes 65552 | tf_op jit(solution)/shard_map/reduce_scatter | solution.py:101
  381.3 0.8 convert_element_type.50
  382.2 5.5 convolution_add_fusion
  387.8 4.5 convolution_bitcast_fusion
  392.3 2.9 convolution_convert_fusion.1
  395.2 0.8 copy.44
  396.0 3.3 convolution_convert_fusion
  399.3 0.8 copy.45
  400.1 39.2 %reduce-scatter.9.cloned.1.call-done = f32[128,1024]{1,0:T(8,128)} async-done(((f32[128,8192]{1,0:T(8,128)}), f32[128,1024]{1,0:T(8,128)}) %reduce-scatter.9.cloned.1.call-update) | async-done | bytes 524304 | tf_op jit(solution)/shard_map/reduce_scatter | solution.py:112
  439.3 1.8 convert_element_type.51
  441.1 157.6 %reduce-scatter.11.cloned.1.call-done = f32[256,256]{0,1:T(8,128)} async-done(((f32[8192,256]{0,1:T(8,128)}), f32[256,256]{0,1:T(8,128)}) %reduce-scatter.11.cloned.1.call-update) | async-done | bytes 262160 | tf_op jit(solution)/shard_map/reduce_scatter | solution.py:118
  598.8 1.0 fusion.46
  599.7 0.8 copy.47
  600.5 0.8 copy.46
  (35 shorter events, 0.4 us)
Async XLA Ops:
  7.2 380.6 %copy-start = (bf16[128,8192]{1,0:T(8,128)(2,1)S(1)}, bf16[128,8192]{1,0:T(8,128)(2,1)}, u32[]{:S(2)}) copy-start(bf16[128,8192]{1,0:T(8,128)(2,1)} %param.16) | copy-start | bytes 6291460
  7.2 86.7 %all-gather.2.cloned.1.call-start = ((), (), s32[]{:S(2)}) async-start(), calls=%async_computation.5 | async-start | bytes 1081344 | tf_op jit(solution)/shard_map/all_gather | solution.py:66
  9.9 85.9 %all-to-all-start = ((bf16[32,128,128]{2,1,0:T(8,128)(2,1)}), bf16[32,128,128]{2,1,0:T(8,128)(2,1)}, u32[]{:S(2)}, u32[]{:S(2)}) async-start(bf16[32,128,128]{2,1,0:T(8,128)(2,1)} %stack.2), calls=%async_computation | async-start | bytes 2097152 | tf_op jit(solution)/shard_map/all_to_all | solution.py:55
  21.3 79.8 %copy-start.7 = (bf16[128,512]{1,0:T(8,128)(2,1)S(1)}, bf16[128,512]{1,0:T(8,128)(2,1)}, u32[]{:S(2)}) copy-start(bf16[128,512]{1,0:T(8,128)(2,1)} %param.10) | copy-start | bytes 393220
  21.4 238.0 %reduce-scatter.5.cloned.1.call-start = ((), (), s32[]{:S(2)}) async-start(), calls=%async_computation.6 | async-start | bytes 2162688 | tf_op jit(solution)/shard_map/reduce_scatter | solution.py:100
  98.7 2.4 copy-start.6
  101.2 21.1 %copy-start.4 = (f32[1,4,128,4096]{2,3,1,0:T(8,128)}, f32[1,4,128,4096]{2,3,1,0:T(8,128)S(1)}, u32[]{:S(2)}) copy-start(f32[1,4,128,4096]{2,3,1,0:T(8,128)S(1)} %get-tuple-element.24) | copy-start | bytes 25165828
  101.2 2.4 copy-start.5
  101.2 2.4 copy-start.10
  102.5 6.2 %copy-start.3 = (f32[1,4,128,4096]{2,3,1,0:T(8,128)}, f32[1,4,128,4096]{2,3,1,0:T(8,128)S(1)}, u32[]{:S(2)}) copy-start(f32[1,4,128,4096]{2,3,1,0:T(8,128)S(1)} %get-tuple-element.20) | copy-start | bytes 25165828
  114.2 8.1 %copy-start.1 = (bf16[4,128,4096]{1,2,0:T(8,128)(2,1)}, bf16[4,128,4096]{1,2,0:T(8,128)(2,1)S(1)}, u32[]{:S(2)}) copy-start(bf16[4,128,4096]{1,2,0:T(8,128)(2,1)S(1)} %fusion.12) | copy-start | bytes 12582916
  114.2 3.8 copy-start.9
  122.3 6.7 %copy-start.8 = (bf16[128,512]{1,0:T(8,128)(2,1)S(1)}, bf16[128,512]{1,0:T(8,128)(2,1)}, u32[]{:S(2)}) copy-start(bf16[128,512]{1,0:T(8,128)(2,1)} %param.12) | copy-start | bytes 393220
  127.1 1.9 copy-start.2
  143.0 238.4 %reduce-scatter.7.cloned.1.call-start = ((), (), s32[]{:S(2)}) async-start(), calls=%async_computation.7 | async-start | bytes 2162688 | tf_op jit(solution)/shard_map/reduce_scatter | solution.py:101
  167.2 272.1 %reduce-scatter.9.cloned.1.call-start = ((), (), s32[]{:S(2)}) async-start(), calls=%async_computation.8 | async-start | bytes 4718592 | tf_op jit(solution)/shard_map/reduce_scatter | solution.py:112
  387.7 211.0 %reduce-scatter.11.cloned.1.call-start = ((), (), s32[]{:S(2)}) async-start(), calls=%async_computation.9 | async-start | bytes 8650752 | tf_op jit(solution)/shard_map/reduce_scatter | solution.py:118
Sparse Core Ops, SparseCore 0:
  10.8 83.0 all-gather.1
  143.1 116.2 reduce-scatter.4
  264.1 117.2 reduce-scatter.6
  387.8 51.4 reduce-scatter.8
  443.6 155.1 reduce-scatter.10
